TPU v7x, 256 devices: a whole 4x4x8 slice. The times are simulated.
256 devices in a mesh: aux: 64 (over y, z, core), orb: 4 (over x).
Axes of the slice: x: 4, y: 4, z: 8, core: 2. Of those that a mesh axis runs over, the one named last changes fastest.
Arguments:
- three_index: bfloat16 [512, 1600, 1600], P('aux', 'orb'), may hold values from -40 to 40, as said below
- density: bfloat16 [512, 1600, 160], P('aux', 'orb'), may hold values from -0.0068359375 to 0.0068359375
- hess_diag: float32 [1440, 160], replicated, may hold values from 0.5 to 4
Outputs:
- ov_new: bfloat16 [4, 512, 57600], P('orb', None, 'aux')
Inputs may be any that keep to these rules, and one draw needn't show every extreme that they name: three_index[q, p, r] equals three_index[q, r, p].
All inputs are finite; a program needn't handle non-finite values.
Results may differ from a plain program's by a relative error of at most 0.0065.
Values may be sent and summed in bfloat16 or wider, within the bound.
A program may use at most 64 MiB of HBM per device.

v0:
```python
import math

import jax
import jax.numpy as jnp
from jax import lax
from jax.sharding import PartitionSpec as P


def on_device(three_index, density, hess_diag):
    highest = lax.Precision.HIGHEST
    aux_count, blk_rows, orb_total = three_index.shape
    n_occ = density.shape[2]
    n_vir = orb_total - n_occ
    orb_pos = lax.axis_index("orb")
    partial_fock = jnp.einsum(
        "qrp,qri->pi", three_index, density, preferred_element_type=jnp.float32
    )[n_occ:]
    radius = math.sqrt(n_occ)
    fock_vo = lax.psum(partial_fock, ("aux", "orb"))
    generator = -fock_vo / hess_diag
    gen_norm = jnp.sqrt(jnp.sum(generator * generator))
    rotation = generator * jnp.minimum(1.0, radius / gen_norm)
    occ_eye = jnp.eye(n_occ, dtype=jnp.float32)
    intersection = jnp.dot(rotation.T, rotation, precision=highest)
    squared = jnp.dot(intersection, intersection, precision=highest)
    rot_over = jnp.dot(rotation, intersection, precision=highest)
    u_occ = jnp.concatenate(
        [occ_eye - intersection / 2.0 + squared / 24.0, rotation - rot_over / 6.0], 0
    )
    left_factor = jnp.concatenate(
        [-(occ_eye - intersection / 6.0), -rotation / 2.0 + rot_over / 24.0], 0
    )
    half_rot = jnp.einsum(
        "qrs,si->qri", three_index, u_occ.astype(jnp.bfloat16), preferred_element_type=jnp.float32
    ).astype(jnp.bfloat16)
    row_start = orb_pos * blk_rows
    rows_factor = lax.dynamic_slice_in_dim(left_factor, row_start, blk_rows, 0)
    row_ids = row_start + lax.broadcasted_iota(jnp.int32, (blk_rows, n_vir), 0)
    col_ids = n_occ + lax.broadcasted_iota(jnp.int32, (blk_rows, n_vir), 1)
    u_vir = (
        jnp.where(row_ids == col_ids, 1.0, 0.0)
        + jnp.dot(rows_factor, rotation.T, precision=highest)
    ).astype(jnp.bfloat16)
    summed = lax.psum_scatter(
        jnp.einsum("qri,ra->iqa", half_rot, u_vir, preferred_element_type=jnp.float32),
        "orb",
        scatter_dimension=0,
        tiled=True,
    )
    rotated = jnp.transpose(summed.astype(jnp.bfloat16), (1, 0, 2))
    pair_block = rotated.reshape(aux_count, -1)
    owned = lax.all_to_all(pair_block, "aux", split_axis=1, concat_axis=0, tiled=True)
    return owned[None]


def solution(mesh):
    return jax.shard_map(
        on_device,
        mesh=mesh,
        in_specs=(P("aux", "orb", None), P("aux", "orb", None), P()),
        out_specs=P("orb", None, "aux"),
        check_vma=False,
    )
```

profile of v0, /device:TPU:1, one launch (start us, length us, event | category | flops | bytes accessed | tf_op | source)
XLA Modules:
  0.0 424.3 jit_solution(3917428919836017234)
XLA Ops:
  6.5 0.0 copy-start
  6.5 0.0 all-reduce.2.cloned.1.call-start
  6.5 1.3 copy-done
  7.9 6.1 %convolution_bitcast_fusion = f32[1600,160]{0,1:T(8,128)S(1)} fusion(bf16[8,400,160]{1,2,0:T(8,128)(2,1)S(1)} %copy-done, bf16[8,400,1600]{2,1,0:T(8,128)(2,1)} %param.3), kind=kOutput, calls=%fused_computation.2 | convolution fusion | flops 1638400000 | bytes 12288000 | tf_op jit(solution)/shard_map/qrp,qri->pi/dot_general | solution.py:15
  14.0 0.0 copy-start.1
  14.0 1.3 slice.4
  15.3 0.0 all-reduce.2.cloned.1.call-update
  15.3 0.2 reduce-scatter.2.cloned.1.call-start
  15.6 257.4 %all-reduce.2.cloned.1.call-done = f32[1440,160]{0,1:T(8,128)} async-done(((f32[1440,160]{0,1:T(8,128)}), f32[1440,160]{0,1:T(8,128)}) %all-reduce.2.cloned.1.call-update) | async-done | bytes 921616 | tf_op jit(solution)/shard_map/psum | solution.py:19
  273.0 0.0 copy-done.1
  273.0 2.1 multiply_reduce_fusion
  275.8 1.0 fusion.15
  276.8 0.3 fusion.2
  277.1 1.2 multiply_add_fusion
  278.3 7.4 %convolution_convert_fusion = bf16[160,8,400]{2,0,1:T(8,128)(2,1)S(1)} fusion(bf16[8,400,1600]{2,1,0:T(8,128)(2,1)} %param.3, bf16[1440,160]{0,1:T(8,128)(2,1)S(1)} %get-tuple-element.8, bf16[160,160]{0,1:T(8,128)(2,1)S(1)} %fusion.2), kind=kOutput, calls=%fused_computation.3 | convolution fusion | flops 1639936000 | bytes 11776000 | tf_op jit(solution)/shard_map/qrs,si->qri/dot_general | solution.py:33
  285.7 2.4 fusion
  288.2 5.3 %fusion.19 = f32[1440,1280]{0,1} fusion(bf16[400,1280]{0,1:T(8,128)(2,1)S(1)} %bitcast.28, bf16[400,1440]{1,0:T(8,128)(2,1)S(1)} %fusion), kind=kOutput, calls=%fused_computation.35 | convolution fusion | flops 1474560000 | bytes 9548800
  293.4 0.0 reduce-scatter.2.cloned.1.call-update
  293.5 79.0 %reduce-scatter.2.cloned.1.call-done = f32[40,8,1440]{2,0,1:T(8,128)} async-done(((f32[160,8,1440]{2,0,1:T(8,128)}), f32[40,8,1440]{2,0,1:T(8,128)}) %reduce-scatter.2.cloned.1.call-update) | async-done | bytes 1843216 | tf_op jit(solution)/shard_map/reduce_scatter | solution.py:44
  372.4 1.6 convert_bitcast_fusion
  374.1 2.5 all_to_all.12
  376.6 0.6 copy.5
  377.2 39.0 %all_to_all.16 = bf16[8,64,900]{2,0,1:T(8,128)(2,1)S(1)} all-to-all(bf16[8,64,900]{2,0,1:T(8,128)(2,1)S(1)} %copy.5), channel_id=1, replica_groups=mesh['aux'=64,'orb'=4] {'aux'}, dimensions={1} | all-to-all | bytes 1843200 | tf_op jit(solution)/shard_map/all_to_all | solution.py:52
  416.2 1.3 copy.6
  (2 shorter events, 0.0 us)
Async XLA Ops:
  6.5 1.3 copy-start
  6.5 266.5 %all-reduce.2.cloned.1.call-start = ((), (), s32[]{:S(2)}) async-start(), calls=%async_computation.2 | async-start | bytes 1966080 | tf_op jit(solution)/shard_map/psum | solution.py:19
  14.0 259.0 %copy-start.1 = (f32[1440,160]{0,1:T(8,128)S(1)}, f32[1440,160]{0,1:T(8,128)}, u32[]{:S(2)}) copy-start(f32[1440,160]{0,1:T(8,128)} %param.5) | copy-start | bytes 2764804
  15.3 357.1 %reduce-scatter.2.cloned.1.call-start = ((), (), s32[]{:S(2)}) async-start(), calls=%async_computation.3 | async-start | bytes 9830400 | tf_op jit(solution)/shard_map/reduce_scatter | solution.py:44
Sparse Core Ops, SparseCore 0:
  15.5 257.4 all-reduce.1
  293.6 78.7 reduce-scatter.1
where the time goes:
time: 425 us; the launch traced here: 424 us
  waiting for transfers between devices  336 us (79%)
  blocking collectives  39 us (9%)
  matrix products  23.8 us (6%)
  between operations  14.2 us (3%)
  local copies, waits for them, and re-layouts  7.02 us (2%)
    psum x1, waiting for transfers between devices, on_device(): fock_vo = lax.psum(partial_fock, ('aux', 'orb'))  257 us
    reduce_scatter x1, waiting for transfers between devices, on_device(): lax.psum_scatter(jnp.einsum('qri,ra->iqa', half_rot, u_vir, preferred_ele...  79 us
    all_to_all x1, blocking collectives, on_device(): lax.all_to_all(pair_block, 'aux', split_axis=1, concat_axis=0, tiled=True)  39 us
  transfers between devices with their start and end apart: 2, of which 2 were waited for; matrix products, arithmetic and copies ran while one was open for 0% of the time, Pallas kernels for 0%

commit v1 on v0

v1 whole, which is shorter than its diff:
```python
import functools
import math

import jax
import jax.numpy as jnp
from jax import lax
from jax.experimental import pallas as pl
from jax.experimental.pallas import tpu as pltpu
from jax.sharding import PartitionSpec as P

MESH = pl.DeviceIdType.MESH
F32 = jnp.float32
BF16 = jnp.bfloat16
NT = (((1,), (1,)), ((), ()))

NO = 160
LANES = 1536
CHIPS = 32
TILES = 15

def place():
    aux = lax.axis_index("aux")
    orb = lax.axis_index("orb")
    return aux, orb, lax.rem(aux, 2), lax.div(aux, 2)


def remote(src, dst, send_sem, recv_sem, aux, orb):
    return pltpu.make_async_remote_copy(
        src_ref=src, dst_ref=dst, send_sem=send_sem, recv_sem=recv_sem,
        device_id={"aux": aux, "orb": orb}, device_id_type=MESH,
    )


def owner_of(tile, core):
    return (2 * tile + core) * 2 + core


def fock_kernel(b_hbm, d_hbm, h_hbm, g_out, bv, dv, hl, hv, acc, cs, cr, xs, xr, ys, yr, g,
                load_sem, cs_sem, cr_sem, xs_sem, xr_sem, ys_sem, yr_sem,
                gs_sem, gr_sem, gxs_sem, gxr_sem, gcs_sem, gcr_sem):
    aux, orb, core, chip = place()
    peer = aux + 1 - 2 * core
    barrier = pltpu.get_barrier_semaphore()

    loads = []
    for q in range(8):
        loads.append((
            pltpu.make_async_copy(d_hbm.at[q], dv.at[q], load_sem.at[2 * q]),
            pltpu.make_async_copy(b_hbm.at[q], bv.at[q], load_sem.at[2 * q + 1]),
        ))
        for copy in loads[-1]:
            copy.start()
    hess_load = pltpu.make_async_copy(h_hbm, hl, load_sem.at[16])
    hess_load.start()

    pl.semaphore_signal(barrier, inc=1, device_id={"aux": peer, "orb": orb}, device_id_type=MESH)
    for step in range(1, 4):
        pl.semaphore_signal(barrier, inc=1, device_id={"aux": aux, "orb": lax.rem(orb + step, 4)},
                            device_id_type=MESH)

    def greet(k, carry):
        other = lax.rem(chip + k, CHIPS) * 2 + core
        pl.semaphore_signal(barrier, inc=1, device_id={"aux": other, "orb": orb}, device_id_type=MESH)
        return carry
    lax.fori_loop(1, CHIPS, greet, 0)

    acc[3, :, 256:384] = jnp.zeros((NO, 128), F32)

    for q in range(8):
        for copy in loads[q]:
            copy.wait()
        part = jnp.dot(dv[q], bv[q, :, 128:1600], preferred_element_type=F32)
        for x in range(4):
            width = 384 if x < 3 else 320
            piece = part[:, 384 * x:384 * x + width]
            if q == 0:
                acc[x, :, :width] = piece
            else:
                acc[x, :, :width] += piece
    hess_load.wait()
    hv[:, 0:1408] = hl[:, 0:1408]
    hv[:, 1408:1536] = jnp.concatenate([hl[:, 1408:1440], jnp.ones((NO, 96), F32)], axis=1)
    pl.semaphore_wait(barrier, 35)

    other_rows = pl.ds(pl.multiple_of(80 * (1 - core), 16), 80)
    my_rows = pl.ds(pl.multiple_of(80 * core, 16), 80)
    core_copies = []
    for x in range(4):
        cs[x] = acc[x, other_rows, :].astype(BF16)
        copy = remote(cs.at[x], cr.at[x], cs_sem.at[x], cr_sem.at[x], peer, orb)
        copy.start()
        core_copies.append(copy)
    for x in range(4):
        core_copies[x].wait_recv()
        xs[x] = (acc[x, my_rows, :] + cr[x].astype(F32)).astype(BF16)
        @pl.when(orb != x)
        def _():
            remote(xs.at[x], xr.at[orb], xs_sem.at[x], xr_sem.at[orb], aux, x).start()
    total = acc[orb, my_rows, :] + cr[orb].astype(F32)
    for step in range(1, 4):
        src = lax.rem(orb + step, 4)
        remote(xs.at[src], xr.at[src], xs_sem.at[src], xr_sem.at[src], aux, src).wait_recv()
        total = total + xr[src].astype(F32)
    for k in range(5):
        for t in range(3):
            ys[3 * k + t] = total[16 * k:16 * k + 16, 128 * t:128 * t + 128].astype(BF16)

    def send_tile(k, carry):
        tile = lax.rem(chip + k, TILES)
        target = owner_of(tile, core)
        @pl.when(target != aux)
        def _():
            remote(ys.at[tile], yr.at[chip], ys_sem.at[tile], yr_sem.at[chip], target, orb).start()
        return carry
    lax.fori_loop(0, TILES, send_tile, 0)

    my_tile = lax.div(chip, 2)
    owner = jnp.logical_and(lax.rem(chip, 2) == core, my_tile < TILES)
    lane_tile = orb * 3 + lax.rem(my_tile, 3)

    @pl.when(owner)
    def _():
        hess_rows = pl.ds(pl.multiple_of(80 * core + 16 * lax.div(my_tile, 3), 16), 16)
        before = hv[hess_rows, pl.ds(pl.multiple_of(jnp.maximum(lane_tile - 1, 0) * 128, 128), 128)]
        after = hv[hess_rows, pl.ds(pl.multiple_of(lane_tile * 128, 128), 128)]
        in_tile = lax.broadcasted_iota(jnp.int32, (16, 128), 1)
        hess = pltpu.roll(jnp.where(in_tile < 96, after, before), 32, 1)
        yr[chip] = ys[my_tile]

        def wait_tile(k, carry):
            src = lax.rem(chip + k, CHIPS)
            remote(ys.at[0], yr.at[src], ys_sem.at[0], yr_sem.at[src], aux, orb).wait_recv()
            return carry
        lax.fori_loop(1, CHIPS, wait_tile, 0)
        fock = yr[0].astype(F32)
        for src in range(1, CHIPS):
            fock = fock + yr[src].astype(F32)
        lane = lane_tile * 128 + in_tile
        valid = jnp.logical_and(lane >= 32, lane < 1472)
        g[core, orb, my_tile] = jnp.where(valid, -fock / hess, 0.0).astype(BF16)

        def spread(k, carry):
            other = lax.rem(chip + k, CHIPS)
            mine = g.at[core, orb, my_tile]
            remote(mine, mine, gs_sem.at[other], gr_sem.at[my_tile], other * 2 + core, orb).start()
            return carry
        lax.fori_loop(1, CHIPS, spread, 0)

    def gather_tile(tile, carry):
        @pl.when(owner_of(tile, core) != aux)
        def _():
            there = g.at[core, orb, tile]
            remote(there, there, gs_sem.at[0], gr_sem.at[tile], aux, orb).wait_recv()
        return carry
    lax.fori_loop(0, TILES, gather_tile, 0)

    own = g.at[core, orb]
    for step in (1, 3, 2):
        x = lax.rem(orb + step, 4)
        remote(own, own, gxs_sem.at[x], gxr_sem.at[orb], aux, x).start()
    remote(own, own, gcs_sem.at[orb], gcr_sem.at[orb], peer, orb).start()
    for step in (1, 3, 2):
        x = lax.rem(orb + step, 4)
        there = g.at[core, x]
        remote(there, there, gxs_sem.at[x], gxr_sem.at[x], aux, x).wait_recv()
        remote(there, there, gcs_sem.at[x], gcr_sem.at[x], peer, orb).start()
    for x in range(4):
        there = g.at[1 - core, x]
        remote(there, there, gcs_sem.at[x], gcr_sem.at[x], peer, orb).wait_recv()
    g_out[...] = g[...]

    for x in range(4):
        core_copies[x].wait_send()
        there = g.at[core, x]
        remote(there, there, gcs_sem.at[x], gcr_sem.at[x], peer, orb).wait_send()
        @pl.when(orb != x)
        def _():
            remote(xs.at[x], xr.at[orb], xs_sem.at[x], xr_sem.at[orb], aux, x).wait_send()
            remote(own, own, gxs_sem.at[x], gxr_sem.at[orb], aux, x).wait_send()

    def sent_tile(tile, carry):
        target = owner_of(tile, core)
        @pl.when(target != aux)
        def _():
            remote(ys.at[tile], yr.at[chip], ys_sem.at[tile], yr_sem.at[chip], target, orb).wait_send()
        return carry
    lax.fori_loop(0, TILES, sent_tile, 0)

    @pl.when(owner)
    def _():
        def sent(k, carry):
            other = lax.rem(chip + k, CHIPS)
            mine = g.at[core, orb, my_tile]
            remote(mine, mine, gs_sem.at[other], gr_sem.at[my_tile], other * 2 + core, orb).wait_send()
            return carry
        lax.fori_loop(1, CHIPS, sent, 0)


def rotate_kernel(g_ref, b_hbm, out, bv, rt, gb, u, left, lx, hs, hb, hr, rot, ob,
                  load_sem, hs_sem, hr_sem, os_sem, or_sem):
    aux, orb, core, chip = place()
    barrier = pltpu.get_barrier_semaphore()
    loads = []
    for q in range(8):
        copy = pltpu.make_async_copy(b_hbm.at[q], bv.at[q], load_sem.at[q])
        copy.start()
        loads.append(copy)

    near = [(0, 1)] + [(step, flip) for step in (1, 3, 2) for flip in (0, 1)]
    def near_device(step, flip):
        other_core = core + flip - 2 * core * flip
        return 2 * chip + other_core, lax.rem(orb + step, 4), other_core
    for step, flip in near:
        to_aux, to_orb, _ = near_device(step, flip)
        pl.semaphore_signal(barrier, inc=1, device_id={"aux": to_aux, "orb": to_orb}, device_id_type=MESH)
    source_core = lax.div(aux, 32)

    def greet(k, carry):
        other = 2 * lax.rem(chip + k, CHIPS) + source_core
        @pl.when(other != aux)
        def _():
            pl.semaphore_signal(barrier, inc=1, device_id={"aux": other, "orb": orb}, device_id_type=MESH)
        return carry
    lax.fori_loop(0, CHIPS, greet, 0)

    for c in range(2):
        for x in range(4):
            for k in range(5):
                for t in range(3):
                    tile = g_ref[c, x, 3 * k + t]
                    lanes = 384 * x + 128 * t
                    gb[80 * c + 16 * k:80 * c + 16 * k + 16, lanes:lanes + 128] = tile
    gb[NO:, :] = jnp.zeros((256 - NO, LANES), BF16)
    gen = gb[0:NO, :].astype(F32)
    norm = jnp.sqrt(jnp.sum(gen * gen, axis=(0, 1), keepdims=True))
    scale = jnp.minimum(1.0, math.sqrt(NO) / norm)
    gram = lax.dot_general(gb[...], gb[...], NT, preferred_element_type=F32)
    inter = gram * (scale * scale)
    inter_b = inter.astype(BF16)
    squared = jnp.dot(inter_b[:NO], inter_b, preferred_element_type=F32)
    over = jnp.dot(inter_b[:NO], gb[...], preferred_element_type=F32) * scale
    rotation = gen * scale
    inter = inter[:NO]
    eye = jnp.where(lax.broadcasted_iota(jnp.int32, (NO, 256), 0)
                    == lax.broadcasted_iota(jnp.int32, (NO, 256), 1), 1.0, 0.0)
    occ = eye - inter / 2.0 + squared / 24.0
    occ_left = inter / 6.0 - eye
    vir = rotation - over / 6.0
    vir_left = over / 24.0 - rotation / 2.0
    early = lax.broadcasted_iota(jnp.int32, (NO, 128), 1) < 32
    u[:, 0:128] = occ[:, 0:128].astype(BF16)
    u[:, 128:256] = jnp.where(early, occ[:, 128:256], vir[:, 0:128]).astype(BF16)
    u[:, 256:1664] = vir[:, 128:1536].astype(BF16)
    left[:, 0:128] = occ_left[:, 0:128]
    left[:, 128:256] = jnp.where(early, occ_left[:, 128:256], vir_left[:, 0:128])
    left[:, 256:1664] = vir_left[:, 128:1536]
    own_lanes = lax.broadcasted_iota(jnp.int32, (NO, 512), 1) < 400
    for x in range(4):
        window = left[:, 384 * x:384 * x + 512]
        if x:
            window = pltpu.roll(window, 512 - 16 * x, 1)
        lx[x] = jnp.where(own_lanes, window, 0.0).astype(BF16)

    pad = jnp.zeros((NO, 112), F32)
    for q in range(8):
        loads[q].wait()
        half = lax.dot_general(u[:, 0:1600], bv[q], NT, preferred_element_type=F32)
        half = jnp.concatenate([half, pad], axis=1)
        for t in range(4):
            hs[t, pl.ds(q, NO, stride=8), :] = half[:, 128 * t:128 * t + 128]
    for t in range(4):
        hb[:, 128 * t:128 * t + 128] = hs[t].astype(BF16)
    waits = 39 - (source_core == core).astype(jnp.int32)
    pl.semaphore_wait(barrier, waits)
    copies = []
    for n, (step, flip) in enumerate(near):
        to_aux, to_orb, to_core = near_device(step, flip)
        rows = pl.ds(pl.multiple_of(160 * (2 * to_orb + to_core), 16), 160)
        copy = remote(hb.at[rows], hr.at[orb, core], hs_sem.at[n], hr_sem.at[2 * orb + core], to_aux, to_orb)
        copy.start()
        copies.append(copy)
    hr[orb, core] = hb[pl.ds(pl.multiple_of(160 * (2 * orb + core), 16), 160), :]
    for step, flip in near:
        _, from_orb, from_core = near_device(step, flip)
        there = hr.at[from_orb, from_core]
        remote(there, there, hs_sem.at[0], hr_sem.at[2 * from_orb + from_core], aux, orb).wait_recv()

    held = [jnp.concatenate([hr[x, 0], hr[x, 1]], axis=0) for x in range(4)]
    mid = lax.dot_general(held[0], lx[0], NT, preferred_element_type=F32)
    for x in range(1, 4):
        mid = mid + lax.dot_general(held[x], lx[x], NT, preferred_element_type=F32)
    rot[...] = jnp.dot((mid * scale).astype(BF16), gb[0:NO, :], preferred_element_type=F32)
    rot[:, 0:384] += held[0][:, 128:512].astype(F32)
    for x, lanes in ((1, 256), (2, 640), (3, 1024)):
        rot[:, lanes:lanes + 512] += pltpu.roll(held[x].astype(F32), 16 * x, 1)

    lane = lax.broadcasted_iota(jnp.int32, (16, 1024), 1)
    for d in range(32):
        j, first = divmod(900 * d, 1440)
        def rows_of(i):
            return jnp.concatenate([rot[8 * i:8 * i + 8, :], rot[160 + 8 * i:168 + 8 * i, :]], axis=0)
        block = pltpu.roll(rows_of(j), LANES - 32 - first, 1)[:, :1024]
        count = min(900, 1440 - first)
        if count < 900:
            block = jnp.where(lane < count, block, pltpu.roll(rows_of(j + 1), count - 32, 1)[:, :1024])
        ob[d] = block.astype(BF16)

    out_rows = pl.ds(pl.multiple_of(16 * chip, 16), 16)

    def send_block(k, carry):
        d = lax.rem(chip + k, 32)
        target = 32 * core + d
        @pl.when(target != aux)
        def _():
            remote(ob.at[d], out.at[out_rows], os_sem.at[d], or_sem.at[chip], target, orb).start()
        @pl.when(target == aux)
        def _():
            pltpu.make_async_copy(ob.at[d], out.at[out_rows], or_sem.at[chip]).start()
        return carry
    lax.fori_loop(0, 32, send_block, 0)

    def land(src, carry):
        rows = pl.ds(pl.multiple_of(16 * src, 16), 16)
        pltpu.make_async_copy(ob.at[0], out.at[rows], or_sem.at[src]).wait()
        return carry
    lax.fori_loop(0, CHIPS, land, 0)

    def sent(d, carry):
        target = 32 * core + d
        @pl.when(target != aux)
        def _():
            remote(ob.at[d], out.at[out_rows], os_sem.at[d], or_sem.at[chip], target, orb).wait_send()
        return carry
    lax.fori_loop(0, 32, sent, 0)
    for copy in copies:
        copy.wait_send()


DMA = pltpu.SemaphoreType.DMA
ANY = pl.BlockSpec(memory_space=pl.ANY)
VM = pl.BlockSpec(memory_space=pltpu.VMEM)


def lay_out_kernel(x_ref, o_ref):
    for t in range(4):
        o_ref[:, 128 * t:128 * t + 128] = x_ref[128 * t:128 * t + 128, :].T[:900]


def on_device(three_index, density, hess_diag):
    gen = pl.pallas_call(
        fock_kernel,
        out_shape=jax.ShapeDtypeStruct((2, 4, TILES, 16, 128), BF16),
        in_specs=[ANY, ANY, ANY],
        out_specs=VM,
        scratch_shapes=[
            pltpu.VMEM((8, 400, 1600), BF16),
            pltpu.VMEM((8, NO, 400), BF16),
            pltpu.VMEM((NO, 1440), F32),
            pltpu.VMEM((NO, LANES), F32),
            pltpu.VMEM((4, NO, 384), F32),
            pltpu.VMEM((4, 80, 384), BF16),
            pltpu.VMEM((4, 80, 384), BF16),
            pltpu.VMEM((4, 80, 384), BF16),
            pltpu.VMEM((4, 80, 384), BF16),
            pltpu.VMEM((TILES, 16, 128), BF16),
            pltpu.VMEM((CHIPS, 16, 128), BF16),
            pltpu.VMEM((2, 4, TILES, 16, 128), BF16),
            DMA((17,)),
            DMA((4,)), DMA((4,)), DMA((4,)), DMA((4,)),
            DMA((TILES,)), DMA((CHIPS,)),
            DMA((CHIPS,)), DMA((TILES,)),
            DMA((4,)), DMA((4,)), DMA((4,)), DMA((4,)),
        ],
        compiler_params=pltpu.CompilerParams(
            collective_id=0, has_side_effects=True, vmem_limit_bytes=60 * 1024 * 1024),
        name="fock_reduce",
    )(three_index, jnp.transpose(density, (0, 2, 1)), hess_diag.T)
    out = pl.pallas_call(
        rotate_kernel,
        out_shape=jax.ShapeDtypeStruct((512, 1024), BF16),
        in_specs=[VM, ANY],
        out_specs=ANY,
        scratch_shapes=[
            pltpu.VMEM((8, 400, 1600), BF16),
            pltpu.VMEM((NO, LANES), F32),
            pltpu.VMEM((256, LANES), BF16),
            pltpu.VMEM((NO, 1664), BF16),
            pltpu.VMEM((NO, 1664), F32),
            pltpu.VMEM((4, NO, 512), BF16),
            pltpu.VMEM((4, 1280, 128), F32),
            pltpu.VMEM((1280, 512), BF16),
            pltpu.VMEM((4, 2, NO, 512), BF16),
            pltpu.VMEM((320, LANES), F32),
            pltpu.VMEM((32, 16, 1024), BF16),
            DMA((8,)),
            DMA((7,)), DMA((8,)),
            DMA((32,)), DMA((CHIPS,)),
        ],
        compiler_params=pltpu.CompilerParams(
            collective_id=1, has_side_effects=True, vmem_limit_bytes=60 * 1024 * 1024),
        name="rotate_exchange",
    )(gen, three_index)
    pairs = pl.pallas_call(
        lay_out_kernel,
        out_shape=jax.ShapeDtypeStruct((900, 512), BF16),
        in_specs=[VM],
        out_specs=VM,
        name="lay_out",
    )(out)
    return pairs.T[None]


def solution(mesh):
    return jax.shard_map(
        on_device,
        mesh=mesh,
        in_specs=(P("aux", "orb", None), P("aux", "orb", None), P()),
        out_specs=P("orb", None, "aux"),
        check_vma=False,
    )
```

time: 425 us -> 95 us (0.22)
  waiting for transfers between devices: 336 us -> 0 us
  Pallas kernels: 0 us -> 94.8 us
  blocking collectives: 39 us -> 0 us
  matrix products: 23.8 us -> 0 us
  between operations: 14.2 us -> 0.02 us
  local copies, waits for them, and re-layouts: 7.02 us -> 0 us
    psum x1 -> x0, waiting for transfers between devices: 257 us -> none  [on_device(): fock_vo = lax.psum(partial_fock, ('aux', 'orb'))]
    pallas_call x0 -> x3, Pallas kernels: none -> 94.8 us  [the longest x1 53.9 us: on_device(): pl.pallas_call(rotate_kernel, out_shape=jax.ShapeDtypeStruct((512, 1024),...]
    reduce_scatter x1 -> x0, waiting for transfers between devices: 79 us -> none  [on_device(): lax.psum_scatter(jnp.einsum('qri,ra->iqa', half_rot, u_vir, preferred_ele...]
    all_to_all x1 -> x0, blocking collectives: 39 us -> none  [on_device(): lax.all_to_all(pair_block, 'aux', split_axis=1, concat_axis=0, tiled=True)]
    dot_general x6 -> x0, matrix products: 18.5 us -> none  [the longest x1 7.39 us: on_device(): jnp.einsum('qrs,si->qri', three_index, u_occ.astype(jnp.bfloat16), prefer...]
    unnamed x1 -> x0, matrix products: 5.28 us -> none
  transfers between devices with their start and end apart: 2 -> 0, of which waited for: 2 -> 0; matrix products, arithmetic and copies ran while one was open for 0% -> 0% of each run, Pallas kernels for 0% -> 0%
where the time goes in v1:
time: 95 us; the launch traced here: 94.8 us
  Pallas kernels  94.8 us (100%)
    pallas_call x1, Pallas kernels, on_device(): pl.pallas_call(rotate_kernel, out_shape=jax.ShapeDtypeStruct((512, 1024),...  53.9 us
    pallas_call x1, Pallas kernels, on_device(): pl.pallas_call(fock_kernel, out_shape=jax.ShapeDtypeStruct((2, 4, TILES,...  38.4 us
    pallas_call x1, Pallas kernels, on_device(): pl.pallas_call(lay_out_kernel, out_shape=jax.ShapeDtypeStruct((900, 512),...  2.48 us

profile of v1, /device:TPU:1, one launch (start us, length us, event | category | flops | bytes accessed | tf_op | source)
XLA Modules:
  0.0 94.8 jit_solution(1987740965365456326)
XLA Ops:
  0.0 38.4 %fock_reduce.1.g_ref = bf16[2,4,15,16,128]{4,3,2,1,0:T(8,128)(2,1)} custom-call(bf16[8,400,1600]{2,1,0:T(8,128)(2,1)} %b_hbm.3, bf16[8,160,400]{2,1,0:T(8,128)(2,1)} %bitcast.5, f32[160,1440]{1,0:T(8,128)} %bitcast.6), custom_call_target="tpu_custom_call" | custom-call | tf_op jit(solution)/shard_map/fock_reduce/pallas_call | solution.py:350
  38.4 53.9 %rotate_exchange.1.x_ref = bf16[512,1024]{1,0:T(8,128)(2,1)} custom-call(bf16[2,4,15,16,128]{4,3,2,1,0:T(8,128)(2,1)} %fock_reduce.1.g_ref, bf16[8,400,1600]{2,1,0:T(8,128)(2,1)} %b_hbm.3), custom_call_target="tpu_custom_call" | custom-call | tf_op jit(solution)/shard_map/rotate_exchange/pallas_call | solution.py:378
  92.3 2.5 %lay_out.1 = bf16[900,512]{1,0:T(8,128)(2,1)} custom-call(bf16[512,1024]{1,0:T(8,128)(2,1)} %rotate_exchange.1.x_ref), custom_call_target="tpu_custom_call" | custom-call | tf_op jit(solution)/shard_map/lay_out/pallas_call | solution.py:403

commit v2 on v1

v2 whole, which is shorter than its diff:
```python
import functools
import math

import jax
import jax.numpy as jnp
from jax import lax
from jax.experimental import pallas as pl
from jax.experimental.pallas import tpu as pltpu
from jax.sharding import PartitionSpec as P

MESH = pl.DeviceIdType.MESH
F32 = jnp.float32
BF16 = jnp.bfloat16
NT = (((1,), (1,)), ((), ()))

NO = 160
LANES = 1536
CHIPS = 32
TILES = 15
PHASES = 2
QP = 8 // PHASES
CUT = 448
FAR_FIRST = sorted(
    ((dy, dz) for dy in range(4) for dz in range(8) if dy or dz),
    key=lambda at: -(min(at[0], 4 - at[0]) + min(at[1], 8 - at[1])),
)


def place():
    aux = lax.axis_index("aux")
    orb = lax.axis_index("orb")
    return aux, orb, lax.rem(aux, 2), lax.div(aux, 2)


def remote(src, dst, send_sem, recv_sem, aux, orb):
    return pltpu.make_async_remote_copy(
        src_ref=src, dst_ref=dst, send_sem=send_sem, recv_sem=recv_sem,
        device_id={"aux": aux, "orb": orb}, device_id_type=MESH,
    )


def owner_of(tile, core):
    return (2 * tile + core) * 2 + core


def kernel(b_hbm, d_hbm, h_hbm, out, bv, dv, hl, hv, acc, cs, cr, xs, xr, ys, yr, g,
           gb, u, left, lx, hs, hb, hr, hx, rot, rc, ob, rv,
           load_sem, cs_sem, cr_sem, xs_sem, xr_sem, ys_sem, yr_sem,
           gs_sem, gr_sem, gxs_sem, gxr_sem, gcs_sem, gcr_sem,
           hs_sem, hr_sem, os_sem, or_sem):
    aux, orb, core, chip = place()
    peer = aux + 1 - 2 * core
    barrier = pltpu.get_barrier_semaphore()

    loads = []
    for q in range(8):
        loads.append((
            pltpu.make_async_copy(d_hbm.at[q], dv.at[q], load_sem.at[2 * q]),
            pltpu.make_async_copy(b_hbm.at[q], bv.at[q], load_sem.at[2 * q + 1]),
        ))
        for copy in loads[-1]:
            copy.start()
    hess_load = pltpu.make_async_copy(h_hbm, hl, load_sem.at[16])
    hess_load.start()

    pl.semaphore_signal(barrier, inc=1, device_id={"aux": peer, "orb": orb}, device_id_type=MESH)
    for step in range(1, 4):
        pl.semaphore_signal(barrier, inc=1, device_id={"aux": aux, "orb": lax.rem(orb + step, 4)},
                            device_id_type=MESH)

    def greet(k, carry):
        other = lax.rem(chip + k, CHIPS) * 2 + core
        pl.semaphore_signal(barrier, inc=1, device_id={"aux": other, "orb": orb}, device_id_type=MESH)
        return carry
    lax.fori_loop(1, CHIPS, greet, 0)

    near = [(0, 1)] + [(step, flip) for step in (1, 3, 2) for flip in (0, 1)]

    def near_device(step, flip):
        other_core = core + flip - 2 * core * flip
        return 2 * chip + other_core, lax.rem(orb + step, 4), other_core
    waits = 35

    g[:, :, TILES] = jnp.zeros((2, 4, 16, 128), BF16)
    acc[3, :, 256:384] = jnp.zeros((NO, 128), F32)

    for q in range(8):
        for copy in loads[q]:
            copy.wait()
        part = jnp.dot(dv[q], bv[q, :, 128:1600], preferred_element_type=F32)
        for x in range(4):
            width = 384 if x < 3 else 320
            piece = part[:, 384 * x:384 * x + width]
            if q == 0:
                acc[x, :, :width] = piece
            else:
                acc[x, :, :width] += piece
    hess_load.wait()
    hv[:, 0:1408] = hl[:, 0:1408]
    hv[:, 1408:1536] = jnp.concatenate([hl[:, 1408:1440], jnp.ones((NO, 96), F32)], axis=1)
    pl.semaphore_wait(barrier, waits)

    other_rows = pl.ds(pl.multiple_of(80 * (1 - core), 16), 80)
    my_rows = pl.ds(pl.multiple_of(80 * core, 16), 80)
    core_copies = []
    for x in range(4):
        cs[x] = acc[x, other_rows, :].astype(BF16)
        copy = remote(cs.at[x], cr.at[x], cs_sem.at[x], cr_sem.at[x], peer, orb)
        copy.start()
        core_copies.append(copy)
    for x in range(4):
        core_copies[x].wait_recv()
        xs[x] = (acc[x, my_rows, :] + cr[x].astype(F32)).astype(BF16)
        @pl.when(orb != x)
        def _():
            remote(xs.at[x], xr.at[orb], xs_sem.at[x], xr_sem.at[orb], aux, x).start()
    total = acc[orb, my_rows, :] + cr[orb].astype(F32)
    for step in range(1, 4):
        src = lax.rem(orb + step, 4)
        remote(xs.at[src], xr.at[src], xs_sem.at[src], xr_sem.at[src], aux, src).wait_recv()
        total = total + xr[src].astype(F32)
    for k in range(5):
        for t in range(3):
            ys[3 * k + t] = total[16 * k:16 * k + 16, 128 * t:128 * t + 128].astype(BF16)

    row, z = lax.div(chip, 8), lax.rem(chip, 8)
    for step_y in (2, 1, 3, 0):
        for step_z in (2, 1, 3, 0):
            tile = 4 * lax.rem(row + step_y, 4) + lax.rem(lax.div(z, 2) + step_z, 4)
            target = owner_of(tile, core)
            @pl.when(jnp.logical_and(tile < TILES, target != aux))
            def _():
                remote(ys.at[tile], yr.at[chip], ys_sem.at[tile], yr_sem.at[chip], target, orb).start()

    my_tile = lax.div(chip, 2)
    owner = jnp.logical_and(lax.rem(chip, 2) == core, my_tile < TILES)
    lane_tile = orb * 3 + lax.rem(my_tile, 3)

    @pl.when(owner)
    def _():
        hess_rows = pl.ds(pl.multiple_of(80 * core + 16 * lax.div(my_tile, 3), 16), 16)
        before = hv[hess_rows, pl.ds(pl.multiple_of(jnp.maximum(lane_tile - 1, 0) * 128, 128), 128)]
        after = hv[hess_rows, pl.ds(pl.multiple_of(lane_tile * 128, 128), 128)]
        in_tile = lax.broadcasted_iota(jnp.int32, (16, 128), 1)
        hess = pltpu.roll(jnp.where(in_tile < 96, after, before), 32, 1)
        yr[chip] = ys[my_tile]

        def wait_tile(k, carry):
            src = lax.rem(chip + k, CHIPS)
            remote(ys.at[0], yr.at[src], ys_sem.at[0], yr_sem.at[src], aux, orb).wait_recv()
            return carry
        lax.fori_loop(1, CHIPS, wait_tile, 0)
        fock = yr[0].astype(F32)
        for src in range(1, CHIPS):
            fock = fock + yr[src].astype(F32)
        lane = lane_tile * 128 + in_tile
        valid = jnp.logical_and(lane >= 32, lane < 1472)
        g[core, orb, my_tile] = jnp.where(valid, -fock / hess, 0.0).astype(BF16)

        mine = g.at[core, orb, my_tile]
        for step_y, step_z in FAR_FIRST:
            other = 8 * lax.rem(row + step_y, 4) + lax.rem(z + step_z, 8)
            remote(mine, mine, gs_sem.at[other], gr_sem.at[my_tile], other * 2 + core, orb).start()

    groups = [lax.rem(row + step, 4) for step in (0, 1, 3, 2)]
    for group in groups:
        for n in range(4):
            tile = 4 * group + n
            @pl.when(jnp.logical_and(tile < TILES, owner_of(tile, core) != aux))
            def _():
                there = g.at[core, orb, tile]
                remote(there, there, gs_sem.at[0], gr_sem.at[tile], aux, orb).wait_recv()
        own = g.at[core, orb, pl.ds(4 * group, 4)]
        for step in (2, 1, 3):
            x = lax.rem(orb + step, 4)
            remote(own, own, gxs_sem.at[x, group], gxr_sem.at[orb, group], aux, x).start()
        remote(own, own, gcs_sem.at[orb, group], gcr_sem.at[orb, group], peer, orb).start()
    for group in groups:
        for step in (1, 3, 2):
            x = lax.rem(orb + step, 4)
            there = g.at[core, x, pl.ds(4 * group, 4)]
            remote(there, there, gxs_sem.at[x, group], gxr_sem.at[x, group], aux, x).wait_recv()
            remote(there, there, gcs_sem.at[x, group], gcr_sem.at[x, group], peer, orb).start()
    for group in groups:
        for step in (0, 1, 3, 2):
            x = lax.rem(orb + step, 4)
            there = g.at[1 - core, x, pl.ds(4 * group, 4)]
            remote(there, there, gcs_sem.at[x, group], gcr_sem.at[x, group], peer, orb).wait_recv()

    for c in range(2):
        for x in range(4):
            for k in range(5):
                for t in range(3):
                    tile = g[c, x, 3 * k + t]
                    lanes = 384 * x + 128 * t
                    gb[80 * c + 16 * k:80 * c + 16 * k + 16, lanes:lanes + 128] = tile
    gb[NO:, :] = jnp.zeros((256 - NO, LANES), BF16)
    gen = gb[0:NO, :].astype(F32)
    norm = jnp.sqrt(jnp.sum(gen * gen, axis=(0, 1), keepdims=True))
    scale = jnp.minimum(1.0, math.sqrt(NO) / norm)
    gram = lax.dot_general(gb[...], gb[...], NT, preferred_element_type=F32)
    inter = gram * (scale * scale)
    inter_b = inter.astype(BF16)
    squared = jnp.dot(inter_b[:NO], inter_b, preferred_element_type=F32)
    over = jnp.dot(inter_b[:NO], gb[...], preferred_element_type=F32) * scale
    rotation = gen * scale
    inter = inter[:NO]
    eye = jnp.where(lax.broadcasted_iota(jnp.int32, (NO, 256), 0)
                    == lax.broadcasted_iota(jnp.int32, (NO, 256), 1), 1.0, 0.0)
    occ = eye - inter / 2.0 + squared / 24.0
    occ_left = inter / 6.0 - eye
    vir = rotation - over / 6.0
    vir_left = over / 24.0 - rotation / 2.0
    early = lax.broadcasted_iota(jnp.int32, (NO, 128), 1) < 32
    u[:, 0:128] = occ[:, 0:128].astype(BF16)
    u[:, 128:256] = jnp.where(early, occ[:, 128:256], vir[:, 0:128]).astype(BF16)
    u[:, 256:1664] = vir[:, 128:1536].astype(BF16)
    left[:, 0:128] = occ_left[:, 0:128]
    left[:, 128:256] = jnp.where(early, occ_left[:, 128:256], vir_left[:, 0:128])
    left[:, 256:1664] = vir_left[:, 128:1536]
    own_lanes = lax.broadcasted_iota(jnp.int32, (NO, 512), 1) < 400
    for x in range(4):
        window = left[:, 384 * x:384 * x + 512]
        if x:
            window = pltpu.roll(window, 512 - 16 * x, 1)
        lx[x] = jnp.where(own_lanes, window, 0.0).astype(BF16)

    pad = jnp.zeros((NO, 112), F32)
    copies = []

    def send_half(p, n):
        to_aux, to_orb, to_core = near_device(*near[n])
        copy = remote(hb.at[p, 2 * to_orb + to_core], hr.at[p, 2 * orb + core], hs_sem.at[p, n],
                      hr_sem.at[p, 2 * orb + core], to_aux, to_orb)
        copy.start()
        copies.append(copy)

    for p in range(PHASES):
        for n in range(QP):
            half = lax.dot_general(u[:, 0:1600], bv[QP * p + n], NT, preferred_element_type=F32)
            half = jnp.concatenate([half, pad], axis=1)
            for t in range(4):
                hs[4 * p + t, pl.ds(n, NO, stride=QP), :] = half[:, 128 * t:128 * t + 128]
        for dest in range(8):
            last = None
            for k in range(5):
                rows = pl.ds(80 * dest + 16 * k, 16)
                for t in range(3):
                    hb[p, dest, 3 * k + t] = hs[4 * p + t, rows, :].astype(BF16)
                piece = hs[4 * p + 3, rows, :]
                last = piece if last is None else last + pltpu.roll(piece, 16 * k, 1)
            hb[p, dest, 15] = last.astype(BF16)
        if p == 0:
            for n in range(7):
                send_half(0, n)
        hr[p, 2 * orb + core] = hb[p, 2 * orb + core]

    tail_lanes = lax.broadcasted_iota(jnp.int32, (16, 128), 1) < 16
    upper = lax.broadcasted_iota(jnp.int32, (8, LANES), 0) < 4
    lane = lax.broadcasted_iota(jnp.int32, (8, 512), 1)

    def block(start, size):
        j, first = divmod(start, 1440)
        count = min(size, 1440 - first)
        low = min((32 + first) // 128 * 128, LANES - 640)
        found = pltpu.roll(rc[j, :, low:low + 640], (640 - 32 - first + low) % 640, 1)[:, :512]
        if count < size:
            more = pltpu.roll(rc[j + 1, :, 0:640], (count - 32) % 640, 1)[:, :512]
            found = jnp.where(lane < count, found, more)
        return found

    def send_block(p, d, near_by):
        target = 32 * core + d

        def go():
            remote(ob.at[p, d], rv.at[p, chip], os_sem.at[p, d], or_sem.at[p, chip], target, orb).start()
        if near_by:
            pl.when(target != aux)(go)
            @pl.when(target == aux)
            def _():
                pltpu.make_async_copy(ob.at[p, d], rv.at[p, chip], or_sem.at[p, chip]).start()
        else:
            go()

    for p in range(PHASES):
        for step, flip in near:
            _, from_orb, from_core = near_device(step, flip)
            there = hr.at[p, 2 * from_orb + from_core]
            remote(there, there, hs_sem.at[p, 0], hr_sem.at[p, 2 * from_orb + from_core], aux, orb).wait_recv()
        for x in range(4):
            for c in range(2):
                last = hr[p, 2 * x + c, 15].astype(F32)
                for k in range(5):
                    rows = pl.ds(80 * c + 16 * k, 16)
                    for t in range(3):
                        hx[x, rows, 128 * t:128 * t + 128] = hr[p, 2 * x + c, 3 * k + t]
                    piece = pltpu.roll(last, (128 - 16 * k) % 128, 1) if k else last
                    hx[x, rows, 384:512] = jnp.where(tail_lanes, piece, 0.0).astype(BF16)
        mid = lax.dot_general(hx[0], lx[0], NT, preferred_element_type=F32)
        for x in range(1, 4):
            mid = mid + lax.dot_general(hx[x], lx[x], NT, preferred_element_type=F32)
        rot[...] = jnp.dot((mid * scale).astype(BF16), gb[0:NO, :], preferred_element_type=F32)
        rot[:, 0:384] += hx[0, :, 128:512].astype(F32)
        for x, lanes in ((1, 256), (2, 640), (3, 1024)):
            rot[:, lanes:lanes + 512] += pltpu.roll(hx[x].astype(F32), 16 * x, 1)
        for m in range(10):
            first_core = rot[8 * m:8 * m + 8, :]
            second_core = rot[80 + 8 * m:88 + 8 * m, :]
            rc[2 * m] = jnp.where(upper, first_core, pltpu.roll(second_core, 4, 0))
            rc[2 * m + 1] = jnp.where(upper, pltpu.roll(first_core, 4, 0), second_core)
        for d in range(32):
            ob[p, d] = jnp.concatenate(
                [block(900 * d, CUT), block(900 * d + CUT, 900 - CUT)], axis=0).astype(BF16)

        for turn, step_z in enumerate((4, 3, 5, 2, 6, 1, 7, 0)):
            if p + 1 < PHASES and turn < 7:
                send_half(p + 1, turn)
            for half_y in range(2):
                for to_core in range(2):
                    d = 16 * half_y + 2 * lax.rem(z + step_z, 8) + to_core
                    send_block(p, d, step_z == 0)

    def lay_out(k, carry):
        group = lax.rem(row + k, 4)

        def land(n, inner):
            for p in range(PHASES):
                there = rv.at[p, 8 * group + n]
                pltpu.make_async_copy(ob.at[p, 0], there, or_sem.at[p, 8 * group + n]).wait()
            return inner
        lax.fori_loop(0, 8, land, 0)
        lanes = pl.ds(pl.multiple_of(128 * group, 128), 128)
        for h in range(2):
            found = []
            for n in range(8):
                early = rv[0, 8 * group + n, 8 * h:8 * h + 8, :].astype(F32)
                late = rv[1, 8 * group + n, 8 * h:8 * h + 8, :].astype(F32)
                found.append(jnp.where(upper[:, :512], early, pltpu.roll(late, 4, 0)))
                found.append(jnp.where(upper[:, :512], pltpu.roll(early, 4, 0), late))
            turned = jnp.concatenate(found, axis=0).T.astype(BF16)
            if h == 0:
                out[0:CUT, lanes] = turned[:CUT]
            else:
                out[CUT:900, lanes] = turned[:900 - CUT]
        return carry
    lax.fori_loop(0, 4, lay_out, 0)

    for x in range(4):
        core_copies[x].wait_send()
        for group in range(4):
            there = g.at[core, x, pl.ds(4 * group, 4)]
            remote(there, there, gcs_sem.at[x, group], gcr_sem.at[x, group], peer, orb).wait_send()
        @pl.when(orb != x)
        def _():
            remote(xs.at[x], xr.at[orb], xs_sem.at[x], xr_sem.at[orb], aux, x).wait_send()
            for group in range(4):
                own = g.at[core, orb, pl.ds(4 * group, 4)]
                remote(own, own, gxs_sem.at[x, group], gxr_sem.at[orb, group], aux, x).wait_send()

    def sent_tile(tile, carry):
        target = owner_of(tile, core)
        @pl.when(target != aux)
        def _():
            remote(ys.at[tile], yr.at[chip], ys_sem.at[tile], yr_sem.at[chip], target, orb).wait_send()
        return carry
    lax.fori_loop(0, TILES, sent_tile, 0)

    @pl.when(owner)
    def _():
        def sent(k, carry):
            other = lax.rem(chip + k, CHIPS)
            mine = g.at[core, orb, my_tile]
            remote(mine, mine, gs_sem.at[other], gr_sem.at[my_tile], other * 2 + core, orb).wait_send()
            return carry
        lax.fori_loop(1, CHIPS, sent, 0)

    def sent_block(d, carry):
        target = 32 * core + d
        @pl.when(target != aux)
        def _():
            for p in range(PHASES):
                remote(ob.at[p, d], rv.at[p, chip], os_sem.at[p, d], or_sem.at[p, chip], target, orb).wait_send()
        return carry
    lax.fori_loop(0, 32, sent_block, 0)
    for copy in copies:
        copy.wait_send()


DMA = pltpu.SemaphoreType.DMA
ANY = pl.BlockSpec(memory_space=pl.ANY)
VM = pl.BlockSpec(memory_space=pltpu.VMEM)


def on_device(three_index, density, hess_diag):
    pairs = pl.pallas_call(
        kernel,
        out_shape=jax.ShapeDtypeStruct((900, 512), BF16),
        in_specs=[ANY, ANY, ANY],
        out_specs=VM,
        scratch_shapes=[
            pltpu.VMEM((8, 400, 1600), BF16),
            pltpu.VMEM((8, NO, 400), BF16),
            pltpu.VMEM((NO, 1440), F32),
            pltpu.VMEM((NO, LANES), F32),
            pltpu.VMEM((4, NO, 384), F32),
            pltpu.VMEM((4, 80, 384), BF16),
            pltpu.VMEM((4, 80, 384), BF16),
            pltpu.VMEM((4, 80, 384), BF16),
            pltpu.VMEM((4, 80, 384), BF16),
            pltpu.VMEM((TILES, 16, 128), BF16),
            pltpu.VMEM((CHIPS, 16, 128), BF16),
            pltpu.VMEM((2, 4, 16, 16, 128), BF16),
            pltpu.VMEM((256, LANES), BF16),
            pltpu.VMEM((NO, 1664), BF16),
            pltpu.VMEM((NO, 1664), F32),
            pltpu.VMEM((4, NO, 512), BF16),
            pltpu.VMEM((4 * PHASES, NO * QP, 128), F32),
            pltpu.VMEM((PHASES, 8, 16, 16, 128), BF16),
            pltpu.VMEM((PHASES, 8, 16, 16, 128), BF16),
            pltpu.VMEM((4, 160, 512), BF16),
            pltpu.VMEM((160, LANES), F32),
            pltpu.VMEM((20, 8, LANES), F32),
            pltpu.VMEM((PHASES, 32, 16, 512), BF16),
            pltpu.VMEM((PHASES, CHIPS, 16, 512), BF16),
            DMA((17,)),
            DMA((4,)), DMA((4,)), DMA((4,)), DMA((4,)),
            DMA((TILES,)), DMA((CHIPS,)),
            DMA((CHIPS,)), DMA((TILES,)),
            DMA((4, 4)), DMA((4, 4)), DMA((4, 4)), DMA((4, 4)),
            DMA((PHASES, 7)), DMA((PHASES, 8)),
            DMA((PHASES, 32)), DMA((PHASES, CHIPS)),
        ],
        compiler_params=pltpu.CompilerParams(
            collective_id=0, has_side_effects=True, vmem_limit_bytes=53 * 1024 * 1024),
        name="rotate",
    )(three_index, jnp.transpose(density, (0, 2, 1)), hess_diag.T)
    return pairs.T[None]


def solution(mesh):
    return jax.shard_map(
        on_device,
        mesh=mesh,
        in_specs=(P("aux", "orb", None), P("aux", "orb", None), P()),
        out_specs=P("orb", None, "aux"),
        check_vma=False,
    )
```

time: 95 us -> 77.4 us (0.81)
  Pallas kernels: 94.8 us -> 76.4 us
    pallas_call x3 -> x1, Pallas kernels: 94.8 us -> 76.4 us  [on_device(): pl.pallas_call(kernel, out_shape=jax.ShapeDtypeStruct((900, 512), BF16),...]
where the time goes in v2:
time: 77.4 us; the launch traced here: 77.3 us
  Pallas kernels  76.4 us (99%)
  local copies, waits for them, and re-layouts  0.93 us (1%)
    pallas_call x1, Pallas kernels, on_device(): pl.pallas_call(kernel, out_shape=jax.ShapeDtypeStruct((900, 512), BF16),...  76.4 us

profile of v2, /device:TPU:1, one launch (start us, length us, event | category | flops | bytes accessed | tf_op | source)
XLA Modules:
  0.0 77.3 jit_solution(3962976133660247343)
XLA Ops:
  0.0 76.4 %rotate.1 = bf16[900,512]{1,0:T(8,128)(2,1)S(1)} custom-call(bf16[8,400,1600]{2,1,0:T(8,128)(2,1)} %b_hbm.1, bf16[8,160,400]{2,1,0:T(8,128)(2,1)} %bitcast.6, f32[160,1440]{1,0:T(8,128)} %bitcast.7), custom_call_target="tpu_custom_call" | custom-call | tf_op jit(solution)/shard_map/rotate/pallas_call | solution.py:395
  76.4 0.9 %copy.5 = bf16[1,512,900]{1,2,0:T(8,128)(2,1)} copy(bf16[1,512,900]{1,2,0:T(8,128)(2,1)S(1)} %bitcast.5) | data formatting | bytes 1843200

commit v3 on v2

--- a/solution.py
+++ b/solution.py
@@ -19,12 +19,6 @@
 TILES = 15
 PHASES = 2
 QP = 8 // PHASES
-CUT = 448
-FAR_FIRST = sorted(
-    ((dy, dz) for dy in range(4) for dz in range(8) if dy or dz),
-    key=lambda at: -(min(at[0], 4 - at[0]) + min(at[1], 8 - at[1])),
-)
-
 
 def place():
     aux = lax.axis_index("aux")
@@ -39,13 +33,9 @@
     )
 
 
-def owner_of(tile, core):
-    return (2 * tile + core) * 2 + core
-
-
-def kernel(b_hbm, d_hbm, h_hbm, out, bv, dv, hl, hv, acc, cs, cr, xs, xr, ys, yr, g,
-           gb, u, left, lx, hs, hb, hr, hx, rot, rc, ob, rv,
-           load_sem, cs_sem, cr_sem, xs_sem, xr_sem, ys_sem, yr_sem,
+def kernel(b_hbm, d_hbm, h_hbm, out, bv, dv, hl, hv, acc, cs, cr, xs, xr, ys, yr, zr, g,
+           gb, u, left, lx, hs, hb, hr, hx, rot, rc, ob, oc, lo, kept, rv, rw, lr, rest_rows,
+           load_sem, cs_sem, cr_sem, xs_sem, xr_sem, ys_sem, yr_sem, zs_sem, zr_sem,
            gs_sem, gr_sem, gxs_sem, gxr_sem, gcs_sem, gcr_sem,
            hs_sem, hr_sem, os_sem, or_sem):
     aux, orb, core, chip = place()
@@ -68,20 +58,21 @@
         pl.semaphore_signal(barrier, inc=1, device_id={"aux": aux, "orb": lax.rem(orb + step, 4)},
                             device_id_type=MESH)
 
-    def greet(k, carry):
-        other = lax.rem(chip + k, CHIPS) * 2 + core
-        pl.semaphore_signal(barrier, inc=1, device_id={"aux": other, "orb": orb}, device_id_type=MESH)
-        return carry
-    lax.fori_loop(1, CHIPS, greet, 0)
-
-    near = [(0, 1)] + [(step, flip) for step in (1, 3, 2) for flip in (0, 1)]
+    for step in range(1, 4):
+        other = lax.rem(lax.div(chip, 8) + step, 4) * 8 + lax.rem(chip, 8)
+        pl.semaphore_signal(barrier, inc=1, device_id={"aux": 2 * other + core, "orb": orb}, device_id_type=MESH)
+    for step in range(1, 8):
+        other = lax.div(chip, 8) * 8 + lax.rem(chip + step, 8)
+        pl.semaphore_signal(barrier, inc=1, device_id={"aux": 2 * other + core, "orb": orb}, device_id_type=MESH)
+
+    near = [(0, 1)] + [(step, flip) for step in (2, 1, 3) for flip in (0, 1)]
 
     def near_device(step, flip):
         other_core = core + flip - 2 * core * flip
         return 2 * chip + other_core, lax.rem(orb + step, 4), other_core
-    waits = 35
 
     g[:, :, TILES] = jnp.zeros((2, 4, 16, 128), BF16)
+    ys[TILES] = jnp.zeros((16, 128), BF16)
     acc[3, :, 256:384] = jnp.zeros((NO, 128), F32)
 
     for q in range(8):
@@ -98,22 +89,25 @@
     hess_load.wait()
     hv[:, 0:1408] = hl[:, 0:1408]
     hv[:, 1408:1536] = jnp.concatenate([hl[:, 1408:1440], jnp.ones((NO, 96), F32)], axis=1)
-    pl.semaphore_wait(barrier, waits)
+    pl.semaphore_wait(barrier, 14)
 
     other_rows = pl.ds(pl.multiple_of(80 * (1 - core), 16), 80)
     my_rows = pl.ds(pl.multiple_of(80 * core, 16), 80)
     core_copies = []
-    for x in range(4):
+    order = [lax.rem(orb + step, 4) for step in (2, 1, 3, 0)]
+    for x in order:
         cs[x] = acc[x, other_rows, :].astype(BF16)
         copy = remote(cs.at[x], cr.at[x], cs_sem.at[x], cr_sem.at[x], peer, orb)
         copy.start()
         core_copies.append(copy)
-    for x in range(4):
-        core_copies[x].wait_recv()
+    x_copies = []
+    for n, x in enumerate(order[:3]):
+        core_copies[n].wait_recv()
         xs[x] = (acc[x, my_rows, :] + cr[x].astype(F32)).astype(BF16)
-        @pl.when(orb != x)
-        def _():
-            remote(xs.at[x], xr.at[orb], xs_sem.at[x], xr_sem.at[orb], aux, x).start()
+        copy = remote(xs.at[x], xr.at[orb], xs_sem.at[x], xr_sem.at[orb], aux, x)
+        copy.start()
+        x_copies.append(copy)
+    core_copies[3].wait_recv()
     total = acc[orb, my_rows, :] + cr[orb].astype(F32)
     for step in range(1, 4):
         src = lax.rem(orb + step, 4)
@@ -124,53 +118,61 @@
             ys[3 * k + t] = total[16 * k:16 * k + 16, 128 * t:128 * t + 128].astype(BF16)
 
     row, z = lax.div(chip, 8), lax.rem(chip, 8)
-    for step_y in (2, 1, 3, 0):
-        for step_z in (2, 1, 3, 0):
-            tile = 4 * lax.rem(row + step_y, 4) + lax.rem(lax.div(z, 2) + step_z, 4)
-            target = owner_of(tile, core)
-            @pl.when(jnp.logical_and(tile < TILES, target != aux))
-            def _():
-                remote(ys.at[tile], yr.at[chip], ys_sem.at[tile], yr_sem.at[chip], target, orb).start()
-
-    my_tile = lax.div(chip, 2)
-    owner = jnp.logical_and(lax.rem(chip, 2) == core, my_tile < TILES)
-    lane_tile = orb * 3 + lax.rem(my_tile, 3)
-
-    @pl.when(owner)
-    def _():
-        hess_rows = pl.ds(pl.multiple_of(80 * core + 16 * lax.div(my_tile, 3), 16), 16)
+    yz_copies = []
+    for step in (2, 1, 3):
+        other = lax.rem(row + step, 4)
+        copy = remote(ys.at[pl.ds(4 * other, 4)], yr.at[row], ys_sem.at[step], yr_sem.at[row],
+                      (8 * other + z) * 2 + core, orb)
+        copy.start()
+        yz_copies.append(copy)
+    yr[row] = ys[pl.ds(4 * row, 4)]
+    for step in (1, 3, 2):
+        src = lax.rem(row + step, 4)
+        remote(yr.at[src], yr.at[src], ys_sem.at[0], yr_sem.at[src], aux, orb).wait_recv()
+    fock = yr[0].astype(F32)
+    for src in range(1, 4):
+        fock = fock + yr[src].astype(F32)
+    zr[z] = fock.astype(BF16)
+
+    for step in (4, 3, 5, 2, 6, 1, 7):
+        far = lax.rem(z + step, 8)
+        copy = remote(zr.at[z], zr.at[z], zs_sem.at[step], zr_sem.at[z], (8 * row + far) * 2 + core, orb)
+        copy.start()
+        yz_copies.append(copy)
+    hess = []
+    in_tile = lax.broadcasted_iota(jnp.int32, (16, 128), 1)
+    for n in range(4):
+        tile = jnp.minimum(4 * row + n, TILES - 1)
+        lane_tile = orb * 3 + lax.rem(tile, 3)
+        hess_rows = pl.ds(pl.multiple_of(80 * core + 16 * lax.div(tile, 3), 16), 16)
         before = hv[hess_rows, pl.ds(pl.multiple_of(jnp.maximum(lane_tile - 1, 0) * 128, 128), 128)]
         after = hv[hess_rows, pl.ds(pl.multiple_of(lane_tile * 128, 128), 128)]
-        in_tile = lax.broadcasted_iota(jnp.int32, (16, 128), 1)
-        hess = pltpu.roll(jnp.where(in_tile < 96, after, before), 32, 1)
-        yr[chip] = ys[my_tile]
-
-        def wait_tile(k, carry):
-            src = lax.rem(chip + k, CHIPS)
-            remote(ys.at[0], yr.at[src], ys_sem.at[0], yr_sem.at[src], aux, orb).wait_recv()
-            return carry
-        lax.fori_loop(1, CHIPS, wait_tile, 0)
-        fock = yr[0].astype(F32)
-        for src in range(1, CHIPS):
-            fock = fock + yr[src].astype(F32)
         lane = lane_tile * 128 + in_tile
         valid = jnp.logical_and(lane >= 32, lane < 1472)
-        g[core, orb, my_tile] = jnp.where(valid, -fock / hess, 0.0).astype(BF16)
-
-        mine = g.at[core, orb, my_tile]
-        for step_y, step_z in FAR_FIRST:
-            other = 8 * lax.rem(row + step_y, 4) + lax.rem(z + step_z, 8)
-            remote(mine, mine, gs_sem.at[other], gr_sem.at[my_tile], other * 2 + core, orb).start()
-
+        hess.append((valid, pltpu.roll(jnp.where(in_tile < 96, after, before), 32, 1)))
+    for step in (1, 7, 2, 6, 3, 5, 4):
+        src = lax.rem(z + step, 8)
+        remote(zr.at[src], zr.at[src], zs_sem.at[0], zr_sem.at[src], aux, orb).wait_recv()
+    for n in range(4):
+        fock = zr[0, n].astype(F32)
+        for src in range(1, 8):
+            fock = fock + zr[src, n].astype(F32)
+        valid, tile_hess = hess[n]
+        @pl.when(4 * row + n < TILES)
+        def _():
+            g[core, orb, 4 * row + n] = jnp.where(valid, -fock / tile_hess, 0.0).astype(BF16)
+
+    own = g.at[core, orb, pl.ds(4 * row, 4)]
+    for step in (2, 1, 3):
+        other = lax.rem(row + step, 4)
+        copy = remote(own, own, gs_sem.at[step], gr_sem.at[row], (8 * other + z) * 2 + core, orb)
+        copy.start()
+        yz_copies.append(copy)
     groups = [lax.rem(row + step, 4) for step in (0, 1, 3, 2)]
-    for group in groups:
-        for n in range(4):
-            tile = 4 * group + n
-            @pl.when(jnp.logical_and(tile < TILES, owner_of(tile, core) != aux))
-            def _():
-                there = g.at[core, orb, tile]
-                remote(there, there, gs_sem.at[0], gr_sem.at[tile], aux, orb).wait_recv()
+    for n, group in enumerate(groups):
         own = g.at[core, orb, pl.ds(4 * group, 4)]
+        if n:
+            remote(own, own, gs_sem.at[0], gr_sem.at[group], aux, orb).wait_recv()
         for step in (2, 1, 3):
             x = lax.rem(orb + step, 4)
             remote(own, own, gxs_sem.at[x, group], gxr_sem.at[orb, group], aux, x).start()
@@ -250,35 +252,41 @@
                 piece = hs[4 * p + 3, rows, :]
                 last = piece if last is None else last + pltpu.roll(piece, 16 * k, 1)
             hb[p, dest, 15] = last.astype(BF16)
-        if p == 0:
-            for n in range(7):
-                send_half(0, n)
+        for n in range(7):
+            send_half(p, n)
         hr[p, 2 * orb + core] = hb[p, 2 * orb + core]
 
     tail_lanes = lax.broadcasted_iota(jnp.int32, (16, 128), 1) < 16
-    upper = lax.broadcasted_iota(jnp.int32, (8, LANES), 0) < 4
-    lane = lax.broadcasted_iota(jnp.int32, (8, 512), 1)
-
-    def block(start, size):
-        j, first = divmod(start, 1440)
-        count = min(size, 1440 - first)
-        low = min((32 + first) // 128 * 128, LANES - 640)
-        found = pltpu.roll(rc[j, :, low:low + 640], (640 - 32 - first + low) % 640, 1)[:, :512]
-        if count < size:
-            more = pltpu.roll(rc[j + 1, :, 0:640], (count - 32) % 640, 1)[:, :512]
-            found = jnp.where(lane < count, found, more)
+    upper = lax.broadcasted_iota(jnp.int32, (8, 128), 0) < 4
+    upper_all = lax.broadcasted_iota(jnp.int32, (8, LANES), 0) < 4
+    lane = lax.broadcasted_iota(jnp.int32, (8, 1024), 1)
+
+    def block(d):
+        j, first = divmod(900 * d, 1440)
+        count = min(900, 1440 - first)
+        found = pltpu.roll(rc[j], (LANES - 32 - first) % LANES, 1)[:, :1024]
+        if count < 900:
+            found = jnp.where(lane < count, found, pltpu.roll(rc[j + 1], (count - 32) % LANES, 1)[:, :1024])
         return found
+
+    def row_of_rest(found, p):
+        rest = jnp.where(lane[:, :128] < 4, found[:, 896:1024], 0.0)
+        return jnp.sum(pltpu.roll(rest, 32 * p, 1, stride=4, stride_axis=0), axis=0, keepdims=True)
 
     def send_block(p, d, near_by):
         target = 32 * core + d
 
+        routes = [(ob.at[d], rv.at[chip])] if p == 0 else [(oc.at[d], rw.at[chip]), (lo.at[d], lr.at[chip])]
+
         def go():
-            remote(ob.at[p, d], rv.at[p, chip], os_sem.at[p, d], or_sem.at[p, chip], target, orb).start()
+            for n, (src, dst) in enumerate(routes):
+                remote(src, dst, os_sem.at[p + n, d], or_sem.at[p + n, chip], target, orb).start()
         if near_by:
             pl.when(target != aux)(go)
             @pl.when(target == aux)
             def _():
-                pltpu.make_async_copy(ob.at[p, d], rv.at[p, chip], or_sem.at[p, chip]).start()
+                for n, (src, dst) in enumerate(routes):
+                    pltpu.make_async_copy(src, dst, or_sem.at[p + n, chip]).start()
         else:
             go()
 
@@ -306,15 +314,19 @@
         for m in range(10):
             first_core = rot[8 * m:8 * m + 8, :]
             second_core = rot[80 + 8 * m:88 + 8 * m, :]
-            rc[2 * m] = jnp.where(upper, first_core, pltpu.roll(second_core, 4, 0))
-            rc[2 * m + 1] = jnp.where(upper, pltpu.roll(first_core, 4, 0), second_core)
+            rc[2 * m] = jnp.where(upper_all, first_core, pltpu.roll(second_core, 4, 0))
+            rc[2 * m + 1] = jnp.where(upper_all, pltpu.roll(first_core, 4, 0), second_core)
         for d in range(32):
-            ob[p, d] = jnp.concatenate(
-                [block(900 * d, CUT), block(900 * d + CUT, 900 - CUT)], axis=0).astype(BF16)
-
+            found = block(d)
+            if p == 0:
+                ob[d] = jnp.concatenate([found[:, 0:384], found[:, 384:768]], axis=0).astype(BF16)
+                kept[d] = found[:, 768:896]
+                lo[d] = row_of_rest(found, 0)
+            else:
+                second = jnp.concatenate([found[:, 512:896], kept[d]], axis=1)
+                oc[d] = jnp.concatenate([found[:, 0:512], second], axis=0).astype(BF16)
+                lo[d] += row_of_rest(found, 1)
         for turn, step_z in enumerate((4, 3, 5, 2, 6, 1, 7, 0)):
-            if p + 1 < PHASES and turn < 7:
-                send_half(p + 1, turn)
             for half_y in range(2):
                 for to_core in range(2):
                     d = 16 * half_y + 2 * lax.rem(z + step_z, 8) + to_core
@@ -324,62 +336,63 @@
         group = lax.rem(row + k, 4)
 
         def land(n, inner):
-            for p in range(PHASES):
-                there = rv.at[p, 8 * group + n]
-                pltpu.make_async_copy(ob.at[p, 0], there, or_sem.at[p, 8 * group + n]).wait()
+            src = 8 * group + n
+            for n, (block_of, there) in enumerate(((ob, rv), (oc, rw), (lo, lr))):
+                pltpu.make_async_copy(block_of.at[0], there.at[src], or_sem.at[n, src]).wait()
+            rest_rows[pl.ds(src, 1), :] = lr[src]
             return inner
         lax.fori_loop(0, 8, land, 0)
         lanes = pl.ds(pl.multiple_of(128 * group, 128), 128)
-        for h in range(2):
+        for t in range(7):
             found = []
             for n in range(8):
-                early = rv[0, 8 * group + n, 8 * h:8 * h + 8, :].astype(F32)
-                late = rv[1, 8 * group + n, 8 * h:8 * h + 8, :].astype(F32)
-                found.append(jnp.where(upper[:, :512], early, pltpu.roll(late, 4, 0)))
-                found.append(jnp.where(upper[:, :512], pltpu.roll(early, 4, 0), late))
-            turned = jnp.concatenate(found, axis=0).T.astype(BF16)
-            if h == 0:
-                out[0:CUT, lanes] = turned[:CUT]
-            else:
-                out[CUT:900, lanes] = turned[:900 - CUT]
+                src = 8 * group + n
+                if t < 3:
+                    early = rv[src, 0:8, 128 * t:128 * t + 128]
+                elif t < 6:
+                    early = rv[src, 8:16, 128 * t - 384:128 * t - 256]
+                else:
+                    early = rw[src, 8:16, 384:512]
+                if t < 4:
+                    late = rw[src, 0:8, 128 * t:128 * t + 128]
+                else:
+                    late = rw[src, 8:16, 128 * t - 512:128 * t - 384]
+                early, late = early.astype(F32), late.astype(F32)
+                found.append(jnp.where(upper, early, pltpu.roll(late, 4, 0)))
+                found.append(jnp.where(upper, pltpu.roll(early, 4, 0), late))
+            out[128 * t:128 * t + 128, lanes] = jnp.concatenate(found, axis=0).T.astype(BF16)
         return carry
     lax.fori_loop(0, 4, lay_out, 0)
 
+    at, turn = lax.broadcasted_iota(jnp.int32, (512, 128), 0), lax.broadcasted_iota(jnp.int32, (512, 128), 1)
+    chips = lax.broadcasted_iota(jnp.int32, (512, 32), 1)
+    spread = jnp.where(lax.broadcasted_iota(jnp.int32, (512, 32), 0) // 16 == chips, 1.0, 0.0).astype(BF16)
+    wide = jnp.dot(spread, rest_rows[...].astype(BF16), preferred_element_type=F32)
+    wanted = 8 * (at // 4 % 2) + 4 * (at // 8 % 2) + at % 4
+    wide = jnp.where(turn // 4 == wanted, wide, 0.0).astype(BF16)
+    column = lax.broadcasted_iota(jnp.int32, (16, 128), 0)
+    pick = jnp.where(lax.broadcasted_iota(jnp.int32, (16, 128), 1) % 4 == column, 1.0, 0.0).astype(BF16)
+    rest = lax.dot_general(pick, wide, NT, preferred_element_type=F32)
+    out[896:900, :] = rest[0:4].astype(BF16)
+
+    for copy in core_copies + x_copies + yz_copies:
+        copy.wait_send()
     for x in range(4):
-        core_copies[x].wait_send()
         for group in range(4):
             there = g.at[core, x, pl.ds(4 * group, 4)]
             remote(there, there, gcs_sem.at[x, group], gcr_sem.at[x, group], peer, orb).wait_send()
         @pl.when(orb != x)
         def _():
-            remote(xs.at[x], xr.at[orb], xs_sem.at[x], xr_sem.at[orb], aux, x).wait_send()
             for group in range(4):
                 own = g.at[core, orb, pl.ds(4 * group, 4)]
                 remote(own, own, gxs_sem.at[x, group], gxr_sem.at[orb, group], aux, x).wait_send()
-
-    def sent_tile(tile, carry):
-        target = owner_of(tile, core)
-        @pl.when(target != aux)
-        def _():
-            remote(ys.at[tile], yr.at[chip], ys_sem.at[tile], yr_sem.at[chip], target, orb).wait_send()
-        return carry
-    lax.fori_loop(0, TILES, sent_tile, 0)
-
-    @pl.when(owner)
-    def _():
-        def sent(k, carry):
-            other = lax.rem(chip + k, CHIPS)
-            mine = g.at[core, orb, my_tile]
-            remote(mine, mine, gs_sem.at[other], gr_sem.at[my_tile], other * 2 + core, orb).wait_send()
-            return carry
-        lax.fori_loop(1, CHIPS, sent, 0)
 
     def sent_block(d, carry):
         target = 32 * core + d
         @pl.when(target != aux)
         def _():
-            for p in range(PHASES):
-                remote(ob.at[p, d], rv.at[p, chip], os_sem.at[p, d], or_sem.at[p, chip], target, orb).wait_send()
+            for n, (src, dst) in enumerate(((ob, rv), (oc, rw), (lo, lr))):
+                remote(src.at[d], dst.at[chip], os_sem.at[n, d], or_sem.at[n, chip], target, orb).wait_send()
         return carry
     lax.fori_loop(0, 32, sent_block, 0)
     for copy in copies:
@@ -407,8 +420,9 @@
             pltpu.VMEM((4, 80, 384), BF16),
             pltpu.VMEM((4, 80, 384), BF16),
             pltpu.VMEM((4, 80, 384), BF16),
-            pltpu.VMEM((TILES, 16, 128), BF16),
-            pltpu.VMEM((CHIPS, 16, 128), BF16),
+            pltpu.VMEM((16, 16, 128), BF16),
+            pltpu.VMEM((4, 4, 16, 128), BF16),
+            pltpu.VMEM((8, 4, 16, 128), BF16),
             pltpu.VMEM((2, 4, 16, 16, 128), BF16),
             pltpu.VMEM((256, LANES), BF16),
             pltpu.VMEM((NO, 1664), BF16),
@@ -420,15 +434,21 @@
             pltpu.VMEM((4, 160, 512), BF16),
             pltpu.VMEM((160, LANES), F32),
             pltpu.VMEM((20, 8, LANES), F32),
-            pltpu.VMEM((PHASES, 32, 16, 512), BF16),
-            pltpu.VMEM((PHASES, CHIPS, 16, 512), BF16),
+            pltpu.VMEM((32, 16, 384), BF16),
+            pltpu.VMEM((32, 16, 512), BF16),
+            pltpu.VMEM((32, 1, 128), F32),
+            pltpu.VMEM((32, 8, 128), F32),
+            pltpu.VMEM((CHIPS, 16, 384), BF16),
+            pltpu.VMEM((CHIPS, 16, 512), BF16),
+            pltpu.VMEM((CHIPS, 1, 128), F32),
+            pltpu.VMEM((CHIPS, 128), F32),
             DMA((17,)),
             DMA((4,)), DMA((4,)), DMA((4,)), DMA((4,)),
-            DMA((TILES,)), DMA((CHIPS,)),
-            DMA((CHIPS,)), DMA((TILES,)),
+            DMA((4,)), DMA((4,)), DMA((8,)), DMA((8,)),
+            DMA((4,)), DMA((4,)),
             DMA((4, 4)), DMA((4, 4)), DMA((4, 4)), DMA((4, 4)),
             DMA((PHASES, 7)), DMA((PHASES, 8)),
-            DMA((PHASES, 32)), DMA((PHASES, CHIPS)),
+            DMA((3, 32)), DMA((3, CHIPS)),
         ],
         compiler_params=pltpu.CompilerParams(
             collective_id=0, has_side_effects=True, vmem_limit_bytes=53 * 1024 * 1024),

time: 77.4 us -> 75.6 us (0.977)
  Pallas kernels: 76.4 us -> 74.6 us
    pallas_call x1, Pallas kernels: 76.4 us -> 74.6 us  [on_device(): pl.pallas_call(kernel, out_shape=jax.ShapeDtypeStruct((900, 512), BF16),...]
where the time goes in v3:
time: 75.6 us; the launch traced here: 75.5 us
  Pallas kernels  74.6 us (99%)
  local copies, waits for them, and re-layouts  0.93 us (1%)
    pallas_call x1, Pallas kernels, on_device(): pl.pallas_call(kernel, out_shape=jax.ShapeDtypeStruct((900, 512), BF16),...  74.6 us

profile of v3, /device:TPU:1, one launch (start us, length us, event | category | flops | bytes accessed | tf_op | source)
XLA Modules:
  0.0 75.5 jit_solution(18257900929674050192)
XLA Ops:
  0.0 74.6 %rotate.1 = bf16[900,512]{1,0:T(8,128)(2,1)S(1)} custom-call(bf16[8,400,1600]{2,1,0:T(8,128)(2,1)} %b_hbm.1, bf16[8,160,400]{2,1,0:T(8,128)(2,1)} %bitcast.6, f32[160,1440]{1,0:T(8,128)} %bitcast.7), custom_call_target="tpu_custom_call" | custom-call | tf_op jit(solution)/shard_map/rotate/pallas_call | solution.py:408
  74.6 0.9 %copy.5 = bf16[1,512,900]{1,2,0:T(8,128)(2,1)} copy(bf16[1,512,900]{1,2,0:T(8,128)(2,1)S(1)} %bitcast.5) | data formatting | bytes 1843200

commit v4 on v3

--- a/solution.py
+++ b/solution.py
@@ -17,6 +17,9 @@
 LANES = 1536
 CHIPS = 32
 TILES = 15
+EARLY = (0, 4, 5, 9, 10, 14, 15, 19)
+ROW_ORDER = EARLY + tuple(n for n in range(20) if n not in EARLY)
+PARTS = ((0, 0, 2, 0), (0, 2, 5, 7), (1, 0, 2, 0), (1, 2, 5, 7))
 PHASES = 2
 QP = 8 // PHASES
 
@@ -217,6 +220,12 @@
     u[:, 0:128] = occ[:, 0:128].astype(BF16)
     u[:, 128:256] = jnp.where(early, occ[:, 128:256], vir[:, 0:128]).astype(BF16)
     u[:, 256:1664] = vir[:, 128:1536].astype(BF16)
+    to_row = lax.broadcasted_iota(jnp.int32, (NO, NO), 0)
+    wanted = jnp.zeros((NO, NO), jnp.int32)
+    for n, i in enumerate(ROW_ORDER):
+        wanted = jnp.where(to_row % 20 == n, to_row - n + i, wanted)
+    order_rows = jnp.where(lax.broadcasted_iota(jnp.int32, (NO, NO), 1) == wanted, 1.0, 0.0).astype(BF16)
+    u[...] = jnp.dot(order_rows, u[...], preferred_element_type=F32).astype(BF16)
     left[:, 0:128] = occ_left[:, 0:128]
     left[:, 128:256] = jnp.where(early, occ_left[:, 128:256], vir_left[:, 0:128])
     left[:, 256:1664] = vir_left[:, 128:1536]
@@ -230,10 +239,15 @@
     pad = jnp.zeros((NO, 112), F32)
     copies = []
 
-    def send_half(p, n):
+    def message(part):
+        p, first, last, tile = PARTS[part]
+        return p, pl.ds(tile, 3 * (last - first) + 1)
+
+    def send_part(part, n):
+        p, tiles = message(part)
         to_aux, to_orb, to_core = near_device(*near[n])
-        copy = remote(hb.at[p, 2 * to_orb + to_core], hr.at[p, 2 * orb + core], hs_sem.at[p, n],
-                      hr_sem.at[p, 2 * orb + core], to_aux, to_orb)
+        copy = remote(hb.at[p, 2 * to_orb + to_core, tiles], hr.at[p, 2 * orb + core, tiles], hs_sem.at[part, n],
+                      hr_sem.at[part, 2 * orb + core], to_aux, to_orb)
         copy.start()
         copies.append(copy)
 
@@ -244,16 +258,19 @@
             for t in range(4):
                 hs[4 * p + t, pl.ds(n, NO, stride=QP), :] = half[:, 128 * t:128 * t + 128]
         for dest in range(8):
-            last = None
-            for k in range(5):
-                rows = pl.ds(80 * dest + 16 * k, 16)
-                for t in range(3):
-                    hb[p, dest, 3 * k + t] = hs[4 * p + t, rows, :].astype(BF16)
-                piece = hs[4 * p + 3, rows, :]
-                last = piece if last is None else last + pltpu.roll(piece, 16 * k, 1)
-            hb[p, dest, 15] = last.astype(BF16)
-        for n in range(7):
-            send_half(p, n)
+            for _, first_group, last_group, tile in [part for part in PARTS if part[0] == p]:
+                tail = None
+                for k in range(first_group, last_group):
+                    rows = pl.ds(80 * dest + 16 * k, 16)
+                    for t in range(3):
+                        hb[p, dest, tile + 3 * (k - first_group) + t] = hs[4 * p + t, rows, :].astype(BF16)
+                    piece = hs[4 * p + 3, rows, :]
+                    tail = piece if tail is None else tail + pltpu.roll(piece, 16 * (k - first_group), 1)
+                hb[p, dest, tile + 3 * (last_group - first_group)] = tail.astype(BF16)
+        for part in range(4):
+            if PARTS[part][0] == p:
+                for n in range(7):
+                    send_part(part, n)
         hr[p, 2 * orb + core] = hb[p, 2 * orb + core]
 
     tail_lanes = lax.broadcasted_iota(jnp.int32, (16, 128), 1) < 16
@@ -290,33 +307,39 @@
         else:
             go()
 
-    for p in range(PHASES):
+    for part, (p, first_group, last_group, tile) in enumerate(PARTS):
+        _, tiles = message(part)
         for step, flip in near:
             _, from_orb, from_core = near_device(step, flip)
-            there = hr.at[p, 2 * from_orb + from_core]
-            remote(there, there, hs_sem.at[p, 0], hr_sem.at[p, 2 * from_orb + from_core], aux, orb).wait_recv()
+            there = hr.at[p, 2 * from_orb + from_core, tiles]
+            remote(there, there, hs_sem.at[part, 0], hr_sem.at[part, 2 * from_orb + from_core], aux, orb).wait_recv()
+        count = 16 * (last_group - first_group)
         for x in range(4):
             for c in range(2):
-                last = hr[p, 2 * x + c, 15].astype(F32)
-                for k in range(5):
-                    rows = pl.ds(80 * c + 16 * k, 16)
+                tail = hr[p, 2 * x + c, tile + 3 * (last_group - first_group)].astype(F32)
+                for k in range(last_group - first_group):
+                    rows = pl.ds(count * c + 16 * k, 16)
                     for t in range(3):
-                        hx[x, rows, 128 * t:128 * t + 128] = hr[p, 2 * x + c, 3 * k + t]
-                    piece = pltpu.roll(last, (128 - 16 * k) % 128, 1) if k else last
+                        hx[x, rows, 128 * t:128 * t + 128] = hr[p, 2 * x + c, tile + 3 * k + t]
+                    piece = pltpu.roll(tail, 128 - 16 * k, 1) if k else tail
                     hx[x, rows, 384:512] = jnp.where(tail_lanes, piece, 0.0).astype(BF16)
-        mid = lax.dot_general(hx[0], lx[0], NT, preferred_element_type=F32)
+        both = pl.ds(0, 2 * count)
+        mid = lax.dot_general(hx[0, both], lx[0], NT, preferred_element_type=F32)
         for x in range(1, 4):
-            mid = mid + lax.dot_general(hx[x], lx[x], NT, preferred_element_type=F32)
-        rot[...] = jnp.dot((mid * scale).astype(BF16), gb[0:NO, :], preferred_element_type=F32)
-        rot[:, 0:384] += hx[0, :, 128:512].astype(F32)
+            mid = mid + lax.dot_general(hx[x, both], lx[x], NT, preferred_element_type=F32)
+        rot[both, :] = jnp.dot((mid * scale).astype(BF16), gb[0:NO, :], preferred_element_type=F32)
+        rot[both, 0:384] += hx[0, both, 128:512].astype(F32)
         for x, lanes in ((1, 256), (2, 640), (3, 1024)):
-            rot[:, lanes:lanes + 512] += pltpu.roll(hx[x].astype(F32), 16 * x, 1)
-        for m in range(10):
+            rot[both, lanes:lanes + 512] += pltpu.roll(hx[x, both].astype(F32), 16 * x, 1)
+        for m in range(count // 8):
             first_core = rot[8 * m:8 * m + 8, :]
-            second_core = rot[80 + 8 * m:88 + 8 * m, :]
-            rc[2 * m] = jnp.where(upper_all, first_core, pltpu.roll(second_core, 4, 0))
-            rc[2 * m + 1] = jnp.where(upper_all, pltpu.roll(first_core, 4, 0), second_core)
+            second_core = rot[count + 8 * m:count + 8 * m + 8, :]
+            at = 4 * first_group + 2 * m
+            rc[ROW_ORDER[at]] = jnp.where(upper_all, first_core, pltpu.roll(second_core, 4, 0))
+            rc[ROW_ORDER[at + 1]] = jnp.where(upper_all, pltpu.roll(first_core, 4, 0), second_core)
         for d in range(32):
+            if (d % 8 in (0, 7)) != (first_group == 0):
+                continue
             found = block(d)
             if p == 0:
                 ob[d] = jnp.concatenate([found[:, 0:384], found[:, 384:768]], axis=0).astype(BF16)
@@ -326,11 +349,20 @@
                 second = jnp.concatenate([found[:, 512:896], kept[d]], axis=1)
                 oc[d] = jnp.concatenate([found[:, 0:512], second], axis=0).astype(BF16)
                 lo[d] += row_of_rest(found, 1)
-        for turn, step_z in enumerate((4, 3, 5, 2, 6, 1, 7, 0)):
+        if first_group == 0:
+            for k in range(4):
+                turn = lax.rem(lax.div(z, 2) + k, 4)
+                for half_y in range(2):
+                    send_block(p, 16 * half_y + 8 * lax.div(turn, 2) + 7 * lax.rem(turn, 2), True)
+            continue
+        for step_z in (4, 3, 5, 2, 6, 1, 7, 0):
             for half_y in range(2):
                 for to_core in range(2):
                     d = 16 * half_y + 2 * lax.rem(z + step_z, 8) + to_core
-                    send_block(p, d, step_z == 0)
+                    whole = lax.rem(d, 8)
+                    @pl.when(jnp.logical_and(whole != 0, whole != 7))
+                    def _():
+                        send_block(p, d, step_z == 0)
 
     def lay_out(k, carry):
         group = lax.rem(row + k, 4)
@@ -348,16 +380,15 @@
             for n in range(8):
                 src = 8 * group + n
                 if t < 3:
-                    early = rv[src, 0:8, 128 * t:128 * t + 128]
+                    early = rv[src, :, 128 * t:128 * t + 128].astype(F32)[0:8]
                 elif t < 6:
-                    early = rv[src, 8:16, 128 * t - 384:128 * t - 256]
+                    early = rv[src, :, 128 * t - 384:128 * t - 256].astype(F32)[8:16]
                 else:
-                    early = rw[src, 8:16, 384:512]
+                    early = rw[src, :, 384:512].astype(F32)[8:16]
                 if t < 4:
-                    late = rw[src, 0:8, 128 * t:128 * t + 128]
+                    late = rw[src, :, 128 * t:128 * t + 128].astype(F32)[0:8]
                 else:
-                    late = rw[src, 8:16, 128 * t - 512:128 * t - 384]
-                early, late = early.astype(F32), late.astype(F32)
+                    late = rw[src, :, 128 * t - 512:128 * t - 384].astype(F32)[8:16]
                 found.append(jnp.where(upper, early, pltpu.roll(late, 4, 0)))
                 found.append(jnp.where(upper, pltpu.roll(early, 4, 0), late))
             out[128 * t:128 * t + 128, lanes] = jnp.concatenate(found, axis=0).T.astype(BF16)
@@ -429,8 +460,8 @@
             pltpu.VMEM((NO, 1664), F32),
             pltpu.VMEM((4, NO, 512), BF16),
             pltpu.VMEM((4 * PHASES, NO * QP, 128), F32),
-            pltpu.VMEM((PHASES, 8, 16, 16, 128), BF16),
-            pltpu.VMEM((PHASES, 8, 16, 16, 128), BF16),
+            pltpu.VMEM((PHASES, 8, 17, 16, 128), BF16),
+            pltpu.VMEM((PHASES, 8, 17, 16, 128), BF16),
             pltpu.VMEM((4, 160, 512), BF16),
             pltpu.VMEM((160, LANES), F32),
             pltpu.VMEM((20, 8, LANES), F32),
@@ -447,7 +478,7 @@
             DMA((4,)), DMA((4,)), DMA((8,)), DMA((8,)),
             DMA((4,)), DMA((4,)),
             DMA((4, 4)), DMA((4, 4)), DMA((4, 4)), DMA((4, 4)),
-            DMA((PHASES, 7)), DMA((PHASES, 8)),
+            DMA((4, 7)), DMA((4, 8)),
             DMA((3, 32)), DMA((3, CHIPS)),
         ],
         compiler_params=pltpu.CompilerParams(

time: 75.6 us -> 74.1 us (0.980)
  Pallas kernels: 74.6 us -> 73.1 us
    pallas_call x1, Pallas kernels: 74.6 us -> 73.1 us  [on_device(): pl.pallas_call(kernel, out_shape=jax.ShapeDtypeStruct((900, 512), BF16),...]
where the time goes in v4:
time: 74.1 us
  Pallas kernels  73.1 us (99%)
  local copies, waits for them, and re-layouts  0.93 us (1%)
    pallas_call x1, Pallas kernels, on_device(): pl.pallas_call(kernel, out_shape=jax.ShapeDtypeStruct((900, 512), BF16),...  73.1 us

profile of v4, /device:TPU:1, one launch (start us, length us, event | category | flops | bytes accessed | tf_op | source)
XLA Modules:
  0.0 74.1 jit_solution(15359052529589420684)
XLA Ops:
  0.0 73.1 %rotate.1 = bf16[900,512]{1,0:T(8,128)(2,1)S(1)} custom-call(bf16[8,400,1600]{2,1,0:T(8,128)(2,1)} %b_hbm.1, bf16[8,160,400]{2,1,0:T(8,128)(2,1)} %bitcast.6, f32[160,1440]{1,0:T(8,128)} %bitcast.7), custom_call_target="tpu_custom_call" | custom-call | tf_op jit(solution)/shard_map/rotate/pallas_call | solution.py:439
  73.1 0.9 %copy.5 = bf16[1,512,900]{1,2,0:T(8,128)(2,1)} copy(bf16[1,512,900]{1,2,0:T(8,128)(2,1)S(1)} %bitcast.5) | data formatting | bytes 1843200

commit v5 on v4

--- a/solution.py
+++ b/solution.py
@@ -257,8 +257,10 @@
             half = jnp.concatenate([half, pad], axis=1)
             for t in range(4):
                 hs[4 * p + t, pl.ds(n, NO, stride=QP), :] = half[:, 128 * t:128 * t + 128]
-        for dest in range(8):
-            for _, first_group, last_group, tile in [part for part in PARTS if part[0] == p]:
+        for part, (half_of, first_group, last_group, tile) in enumerate(PARTS):
+            if half_of != p:
+                continue
+            for dest in range(8):
                 tail = None
                 for k in range(first_group, last_group):
                     rows = pl.ds(80 * dest + 16 * k, 16)
@@ -267,10 +269,8 @@
                     piece = hs[4 * p + 3, rows, :]
                     tail = piece if tail is None else tail + pltpu.roll(piece, 16 * (k - first_group), 1)
                 hb[p, dest, tile + 3 * (last_group - first_group)] = tail.astype(BF16)
-        for part in range(4):
-            if PARTS[part][0] == p:
-                for n in range(7):
-                    send_part(part, n)
+            for n in range(7):
+                send_part(part, n)
         hr[p, 2 * orb + core] = hb[p, 2 * orb + core]
 
     tail_lanes = lax.broadcasted_iota(jnp.int32, (16, 128), 1) < 16
@@ -290,20 +290,17 @@
         rest = jnp.where(lane[:, :128] < 4, found[:, 896:1024], 0.0)
         return jnp.sum(pltpu.roll(rest, 32 * p, 1, stride=4, stride_axis=0), axis=0, keepdims=True)
 
-    def send_block(p, d, near_by):
+    def send_block(kind, d, near_by):
         target = 32 * core + d
-
-        routes = [(ob.at[d], rv.at[chip])] if p == 0 else [(oc.at[d], rw.at[chip]), (lo.at[d], lr.at[chip])]
+        source, landing = ((ob, rv), (oc, rw), (lo, lr))[kind]
 
         def go():
-            for n, (src, dst) in enumerate(routes):
-                remote(src, dst, os_sem.at[p + n, d], or_sem.at[p + n, chip], target, orb).start()
+            remote(source.at[d], landing.at[chip], os_sem.at[kind, d], or_sem.at[kind, chip], target, orb).start()
         if near_by:
             pl.when(target != aux)(go)
             @pl.when(target == aux)
             def _():
-                for n, (src, dst) in enumerate(routes):
-                    pltpu.make_async_copy(src, dst, or_sem.at[p + n, chip]).start()
+                pltpu.make_async_copy(source.at[d], landing.at[chip], or_sem.at[kind, chip]).start()
         else:
             go()
 
@@ -364,6 +361,11 @@
                     def _():
                         send_block(p, d, step_z == 0)
 
+    for step_z in (4, 3, 5, 2, 6, 1, 7, 0):
+        for half_y in range(2):
+            for to_core in range(2):
+                send_block(2, 16 * half_y + 2 * lax.rem(z + step_z, 8) + to_core, step_z == 0)
+
     def lay_out(k, carry):
         group = lax.rem(row + k, 4)
 

time: 74.1 us -> 76 us (1.026)
  Pallas kernels: 73.1 us -> 75 us
    pallas_call x1, Pallas kernels: 73.1 us -> 75 us  [on_device(): pl.pallas_call(kernel, out_shape=jax.ShapeDtypeStruct((900, 512), BF16),...]
where the time goes in v5:
time: 76 us; the launch traced here: 75.9 us
  Pallas kernels  75 us (99%)
  local copies, waits for them, and re-layouts  0.93 us (1%)
    pallas_call x1, Pallas kernels, on_device(): pl.pallas_call(kernel, out_shape=jax.ShapeDtypeStruct((900, 512), BF16),...  75 us

profile of v5, /device:TPU:1, one launch (start us, length us, event | category | flops | bytes accessed | tf_op | source)
XLA Modules:
  0.0 75.9 jit_solution(10075664364555516289)
XLA Ops:
  0.0 75.0 %rotate.1 = bf16[900,512]{1,0:T(8,128)(2,1)S(1)} custom-call(bf16[8,400,1600]{2,1,0:T(8,128)(2,1)} %b_hbm.1, bf16[8,160,400]{2,1,0:T(8,128)(2,1)} %bitcast.6, f32[160,1440]{1,0:T(8,128)} %bitcast.7), custom_call_target="tpu_custom_call" | custom-call | tf_op jit(solution)/shard_map/rotate/pallas_call | solution.py:441
  75.0 0.9 %copy.5 = bf16[1,512,900]{1,2,0:T(8,128)(2,1)} copy(bf16[1,512,900]{1,2,0:T(8,128)(2,1)S(1)} %bitcast.5) | data formatting | bytes 1843200
